TPU v7x, 256 devices: a whole 4x4x8 slice. The times are simulated.
256 devices in a mesh: scen: 32 (over y, x, core), col: 8 (over z).
Axes of the slice: x: 4, y: 4, z: 8, core: 2. Of those that a mesh axis runs over, the one named last changes fastest.
Arguments:
- inverses: float32 [32, 1024, 1024], P('scen'), as said below
- coupling: float32 [32, 1024, 8192], P('scen', None, 'col'), may hold values from -0.1875 to 0.1875
- tile_mask: int32 [32, 8], P('scen'), may hold values 0 or 1
- hess_diag: float32 [512], replicated, may hold values from 1 to 16
Outputs:
- factor: float32 [8192, 512], P(('col', 'scen'))
Inputs may be any that keep to these rules, and one draw needn't show every extreme that they name: `inverses`: each scenario's matrix is symmetric and positive definite.
All inputs are finite; a program needn't handle non-finite values. No bound on the sum of `tile_mask` on one device may be relied on, other than what follows from the above.
Results may differ from a plain program's by a relative error of at most 0.0001.
Values sent between devices are 32-bit elements; how exact they have to be, the bound alone decides.
A program may use at most 64 MiB of HBM per device.

v0:
```python
import jax
import jax.numpy as jnp
from jax import lax
from jax.sharding import PartitionSpec as P


def filled_up(lines, size):
    spare = -lines.shape[0] % size
    if not spare:
        return lines
    return jnp.concatenate([lines, jnp.zeros((spare, *lines.shape[1:]), lines.dtype)])


def spread(x, axis, root):
    lines = jnp.where(lax.axis_index(axis) == root, x, jnp.zeros_like(x)).reshape(
        -1, *x.shape[1:][-1:]
    )
    padded = filled_up(lines, lax.axis_size(axis))
    own = lax.psum_scatter(padded, axis, scatter_dimension=0, tiled=True)
    return lax.all_gather(own, axis, axis=0, tiled=True)[: len(lines)].reshape(x.shape)


def in_blocks(x, dim, size):
    lengths = x.shape
    blocks = x.reshape(*lengths[:dim], size, lengths[dim] // size, *lengths[dim + 1 :])
    return jnp.moveaxis(blocks, dim, 0)


def sum_at_owner(x, axis, dim):
    size = lax.axis_size(axis)
    blocks = lax.all_to_all(in_blocks(x, dim, size), axis, 0, 0, tiled=True)
    return jnp.sum(blocks, axis=0)


def sent_to_all(x, axis):
    size = lax.axis_size(axis)
    return lax.all_to_all(jnp.broadcast_to(x[None], (size, *x.shape)), axis, 0, 0, tiled=True)


def in_order(blocks, dim):
    lengths = list(blocks.shape[1:])
    lengths[dim] *= blocks.shape[0]
    return jnp.moveaxis(blocks, 0, dim).reshape(lengths)


def collect(x, axis, dim):
    blocks = sent_to_all(x, axis)
    return in_order(blocks, dim)


def from_root(x, axis, root):
    return lax.dynamic_index_in_dim(lax.all_gather(x, axis), root, 0, keepdims=False)


def outer_rows(left, piece):
    return lax.dot_general(
        left,
        piece,
        (((0,), (0,)), ((), ())),
        precision=lax.Precision.HIGHEST,
        preferred_element_type=jnp.float32,
    )


def matmul(left, right):
    return jnp.dot(left, right, precision=lax.Precision.HIGHEST, preferred_element_type=jnp.float32)


def body(inverses, coupling, tile_mask, hess_diag):
    inverse = inverses[0]
    local = coupling[0]
    width = hess_diag.shape[0]
    half = width // 2
    scen_size = lax.axis_size("scen")
    rows = local.shape[1] // scen_size
    row_keep = jnp.repeat(tile_mask[0].astype(jnp.float32), local.shape[0] // tile_mask.shape[1])
    panel = spread(local[:, :width], "col", 0)
    panel = panel * row_keep[:, None]
    product = matmul(inverse, panel) * row_keep[:, None]
    block = local
    summed = sum_at_owner(outer_rows(block, product), "scen", 0)
    first = lax.axis_index("col") * local.shape[1] + lax.axis_index("scen") * rows
    global_rows = first + jnp.arange(rows, dtype=jnp.int32)
    columns = jnp.arange(width, dtype=jnp.int32)
    schur = summed + jnp.where(columns[None, :] == global_rows[:, None], hess_diag[None, :], 0.0)

    def fetch(stacked, low):
        whole = collect(stacked, "scen", 1)
        block = whole[:, low : low + half]
        return from_root(block, "col", 0)

    identity = jnp.eye(half, dtype=jnp.float32)
    block_one = fetch(schur[None, :, :half], 0)[0]
    chol1 = jnp.linalg.cholesky(block_one)
    inv1 = jax.scipy.linalg.solve_triangular(chol1, identity, lower=True)
    lcol1 = matmul(schur[:, :half], inv1.T)
    own_one = lax.dynamic_slice_in_dim(chol1, jnp.clip(first, 0, half - rows), rows, 0)
    lcol1 = jnp.where(first < half, own_one, lcol1)
    paired = fetch(jnp.stack([schur[:, half:], lcol1]), half)
    lower_b = paired[1]
    update = paired[0] - matmul(lower_b, lower_b.T)
    chol2 = jnp.linalg.cholesky(update)
    inv2 = jax.scipy.linalg.solve_triangular(chol2, identity, lower=True)
    remain = schur[:, half:] - matmul(lcol1, lower_b.T)
    lcol2 = matmul(remain, inv2.T)
    own_two = lax.dynamic_slice_in_dim(chol2, jnp.clip(first - half, 0, half - rows), rows, 0)
    lcol2 = jnp.where(first < width, own_two, lcol2)
    lcol2 = jnp.where(first < half, jnp.zeros_like(lcol2), lcol2)
    return jnp.concatenate([lcol1, lcol2], axis=1)


def solution(mesh):
    in_specs = (P("scen", None, None), P("scen", None, "col"), P("scen", None), P())
    out_specs = P(("col", "scen"), None)
    return jax.shard_map(body, mesh=mesh, in_specs=in_specs, out_specs=out_specs, check_vma=False)
```

profile of v0, /device:TPU:6, one launch (start us, length us, event | category | flops | bytes accessed | tf_op | source)
XLA Modules:
  0.0 445.0 jit_solution(16157020041369222814)
XLA Ops:
  6.5 3.2 slice_select_fusion
  9.8 45.4 %reduce-scatter.2.cloned.1.call-done = f32[128,512]{1,0:T(8,128)} async-done(((f32[1024,512]{1,0:T(8,128)}), f32[128,512]{1,0:T(8,128)}) %reduce-scatter.2.cloned.1.call-update) | async-done | bytes 262160 | tf_op jit(solution)/shard_map/reduce_scatter | solution.py:19
  55.3 41.4 %all-gather.6.cloned.1.call-done = f32[1024,512]{1,0:T(8,128)} async-done(((f32[128,512]{1,0:T(8,128)}), f32[1024,512]{1,0:T(8,128)}) %all-gather.6.cloned.1.call-update) | async-done | bytes 2097168 | tf_op jit(solution)/shard_map/all_gather | solution.py:20
  96.7 16.9 %fusion = f32[512,1024]{1,0:T(8,128)S(1)} fusion(f32[1,1024,1024]{2,1,0:T(8,128)} %param.7, f32[1024,512]{1,0:T(8,128)} %all-gather.6.cloned.1.call-done, f32[1024]{0:T(1024)S(1)} %broadcast_bitcast_fusion), kind=kOutput, calls=%fused_computation.4 | convolution fusion | flops 6442975232 | bytes 8392704 | tf_op jit(solution)/shard_map/dot_general | solution.py:66
  113.6 6.9 %fusion.5 = f32[1024,512]{0,1:T(8,128)S(1)} fusion(f32[512,1024]{1,0:T(8,128)S(1)} %fusion, f32[1024]{0:T(1024)S(1)} %broadcast_bitcast_fusion, f32[1,1024,1024]{2,1,0:T(8,128)S(1)} %copy-done), kind=kOutput, calls=%fused_computation.10 | convolution fusion | flops 6442975232 | bytes 8392704 | tf_op jit(solution)/shard_map/dot_general | solution.py:56
  120.5 1.9 copy.16
  122.3 7.4 %all-to-all-start = ((f32[32,32,512]{2,1,0:T(8,128)}), f32[32,32,512]{2,1,0:T(8,128)S(1)}, u32[]{:S(2)}, u32[]{:S(2)}) async-start(f32[32,32,512]{2,1,0:T(8,128)} %bitcast.98), calls=%async_computation.1 | async-start | bytes 4194304 | tf_op jit(solution)/shard_map/all_to_all | solution.py:31
  129.8 25.5 %all-to-all-done = f32[32,32,512]{2,1,0:T(8,128)S(1)} async-done(((f32[32,32,512]{2,1,0:T(8,128)}), f32[32,32,512]{2,1,0:T(8,128)S(1)}, u32[]{:S(2)}, u32[]{:S(2)}) %all-to-all-start) | async-done | bytes 2097184 | tf_op jit(solution)/shard_map/all_to_all | solution.py:31
  155.7 22.1 %all_to_all.15 = f32[32,1,32,256]{3,2,1,0:T(8,128)S(1)} all-to-all(f32[32,1,32,256]{3,2,1,0:T(8,128)S(1)} %broadcast_in_dim.40), channel_id=1, replica_groups=mesh['scen'=32,'col'=8] {'scen'}, dimensions={0} | all-to-all | bytes 2097152 | tf_op jit(solution)/shard_map/all_to_all | solution.py:37
  178.8 38.4 %all-gather.8.cloned.1.call-done = f32[8,256,256]{2,1,0:T(8,128)} async-done(((f32[1,256,256]{2,1,0:T(8,128)}), f32[8,256,256]{2,1,0:T(8,128)}) %all-gather.8.cloned.1.call-update) | async-done | bytes 2097168 | tf_op jit(solution)/shard_map/all_gather | solution.py:52
  219.3 11.7 %cholesky.130 = f32[128,128]{1,0:T(8,128)S(1)} custom-call(f32[128,128]{1,0:T(8,128)S(1)} %cholesky.194), custom_call_target="Cholesky" | custom-call | tf_op jit(solution)/shard_map/jit(cholesky)/cholesky | solution.py:94
  231.0 9.8 %custom-call.13 = f32[1,128,128]{1,2,0:T(8,128)S(1)} custom-call(f32[1,128,128]{2,1,0:T(8,128)S(1)} %get-tuple-element.56), custom_call_target="InvertDiagBlocksLowerTriangular" | custom-call | tf_op jit(solution)/shard_map/jit(cholesky)/cholesky | solution.py:94
  241.3 11.7 %cholesky.147 = f32[128,128]{1,0:T(8,128)S(1)} custom-call(f32[128,128]{1,0:T(8,128)S(1)} %convolution_subtract_fusion.4), custom_call_target="Cholesky" | custom-call | tf_op jit(solution)/shard_map/jit(cholesky)/cholesky | solution.py:94
  255.2 4.0 while.4
  259.2 19.7 %custom-call.14 = f32[2,128,128]{1,2,0:T(8,128)S(1)} custom-call(f32[2,128,128]{2,1,0:T(8,128)S(1)} %get-tuple-element.21), custom_call_target="InvertDiagBlocksLowerTriangular" | custom-call | tf_op jit(solution)/shard_map/jit(_solve_triangular)/triangular_solve | solution.py:95
  280.4 33.4 %all_to_all.16 = f32[32,2,32,256]{3,2,1,0:T(8,128)S(1)} all-to-all(f32[32,2,32,256]{3,2,1,0:T(8,128)S(1)} %broadcast_in_dim.42), channel_id=1, replica_groups=mesh['scen'=32,'col'=8] {'scen'}, dimensions={0} | all-to-all | bytes 4194304 | tf_op jit(solution)/shard_map/all_to_all | solution.py:37
  315.0 52.2 %all-gather.10.cloned.1.call-done = f32[16,256,256]{2,1,0:T(8,128)} async-done(((f32[2,256,256]{2,1,0:T(8,128)}), f32[16,256,256]{2,1,0:T(8,128)}) %all-gather.10.cloned.1.call-update) | async-done | bytes 4194320 | tf_op jit(solution)/shard_map/all_gather | solution.py:52
  367.2 5.4 %copy.20 = f32[16,256,256]{1,2,0:T(8,128)} copy(f32[16,256,256]{2,1,0:T(8,128)} %all-gather.10.cloned.1.call-done) | data formatting | bytes 8388608 | tf_op jit(solution)/shard_map/all_gather | solution.py:52
  372.6 1.7 convolution_subtract_fusion
  375.6 11.7 %cholesky.164 = f32[128,128]{1,0:T(8,128)S(1)} custom-call(f32[128,128]{1,0:T(8,128)S(1)} %cholesky.197), custom_call_target="Cholesky" | custom-call | tf_op jit(solution)/shard_map/jit(cholesky)/cholesky | solution.py:102
  387.4 9.8 %custom-call.15 = f32[1,128,128]{1,2,0:T(8,128)S(1)} custom-call(f32[1,128,128]{2,1,0:T(8,128)S(1)} %get-tuple-element.50), custom_call_target="InvertDiagBlocksLowerTriangular" | custom-call | tf_op jit(solution)/shard_map/jit(cholesky)/cholesky | solution.py:102
  397.7 11.7 %cholesky.181 = f32[128,128]{1,0:T(8,128)S(1)} custom-call(f32[128,128]{1,0:T(8,128)S(1)} %convolution_subtract_fusion.3), custom_call_target="Cholesky" | custom-call | tf_op jit(solution)/shard_map/jit(cholesky)/cholesky | solution.py:102
  412.2 4.0 while.5
  416.2 19.9 %custom-call.16 = f32[2,128,128]{1,2,0:T(8,128)S(1)} custom-call(f32[2,128,128]{2,1,0:T(8,128)S(1)} %get-tuple-element.22), custom_call_target="InvertDiagBlocksLowerTriangular" | custom-call | tf_op jit(solution)/shard_map/jit(_solve_triangular)/triangular_solve | solution.py:103
  (75 shorter events, 20.7 us)
Async XLA Ops:
  6.5 48.6 %reduce-scatter.2.cloned.1.call-start = ((), (), s32[]{:S(2)}) async-start(), calls=%async_computation.4 | async-start | bytes 2359296 | tf_op jit(solution)/shard_map/reduce_scatter | solution.py:19
  9.7 45.5 %copy-start.2 = (s32[1,8]{1,0:T(1,128)S(1)}, s32[1,8]{1,0:T(1,128)}, u32[]{:S(2)}) copy-start(s32[1,8]{1,0:T(1,128)} %param.9) | copy-start | bytes 100
  9.7 87.0 %all-gather.6.cloned.1.call-start = ((), (), s32[]{:S(2)}) async-start(), calls=%async_computation.5 | async-start | bytes 2359296 | tf_op jit(solution)/shard_map/all_gather | solution.py:20
  96.7 16.9 %copy-start = (f32[1,1024,1024]{2,1,0:T(8,128)S(1)}, f32[1,1024,1024]{2,1,0:T(8,128)}, u32[]{:S(2)}) copy-start(f32[1,1024,1024]{2,1,0:T(8,128)} %param.8) | copy-start | bytes 12582916
  122.3 33.0 %all-to-all-start = ((f32[32,32,512]{2,1,0:T(8,128)}), f32[32,32,512]{2,1,0:T(8,128)S(1)}, u32[]{:S(2)}, u32[]{:S(2)}) async-start(f32[32,32,512]{2,1,0:T(8,128)} %bitcast.98), calls=%async_computation.1 | async-start | bytes 4194304 | tf_op jit(solution)/shard_map/all_to_all | solution.py:31
  129.7 25.7 %copy-start.1 = (f32[512]{0:T(512)S(1)}, f32[512]{0:T(512)}, u32[]{:S(2)}) copy-start(f32[512]{0:T(512)} %param.10) | copy-start | bytes 6148
  129.7 87.4 %all-gather.8.cloned.1.call-start = ((), (), s32[]{:S(2)}) async-start(), calls=%async_computation.6 | async-start | bytes 2359296 | tf_op jit(solution)/shard_map/all_gather | solution.py:52
  178.5 188.7 %all-gather.10.cloned.1.call-start = ((), (), s32[]{:S(2)}) async-start(), calls=%async_computation.7 | async-start | bytes 4718592 | tf_op jit(solution)/shard_map/all_gather | solution.py:52
Sparse Core Ops, SparseCore 0:
  9.9 45.2 reduce-scatter.1
  57.0 39.6 all-gather.5
  178.6 38.4 all-gather.7
  315.1 52.0 all-gather.9
where the time goes:
time: 452 us; the launch traced here: 445 us
  waiting for transfers between devices  203 us (45%)
  other arithmetic  113 us (25%)
  blocking collectives  55.5 us (12%)
  matrix products  30 us (7%)
  local copies, waits for them, and re-layouts  18.7 us (4%)
  between operations  16.5 us (4%)
  starting transfers between devices  7.7 us (2%)
    all_gather x2, waiting for transfers between devices, from_root(): lax.all_gather(x, axis)  90.6 us
    all_to_all x2, blocking collectives, sent_to_all(): lax.all_to_all(jnp.broadcast_to(x[None], (size, *x.shape)), axis, 0, 0, t...  55.5 us
    reduce_scatter x1, waiting for transfers between devices, spread(): own = lax.psum_scatter(padded, axis, scatter_dimension=0, tiled=True)  45.4 us
    all_gather x1, waiting for transfers between devices, spread(): lax.all_gather(own, axis, axis=0, tiled=True)[:len(lines)].reshape(x.shape)  41.4 us
    another operation x7, other arithmetic, body(): chol2 = jnp.linalg.cholesky(update)  34.7 us
    another operation x6, other arithmetic, body(): chol1 = jnp.linalg.cholesky(block_one)  34 us
    all_to_all x1, waiting for transfers between devices, sum_at_owner(): blocks = lax.all_to_all(in_blocks(x, dim, size), axis, 0, 0, tiled=True)  25.5 us
    dot_general x5, matrix products, matmul(): jnp.dot(left, right, precision=lax.Precision.HIGHEST, preferred_element_t...  20.4 us
  transfers between devices with their start and end apart: 5, of which 5 were waited for; matrix products, arithmetic and copies ran while one was open for 0% of the time, Pallas kernels for 0%

commit v1 on v0

--- a/solution.py
+++ b/solution.py
@@ -1,6 +1,10 @@
+import functools
+
 import jax
 import jax.numpy as jnp
 from jax import lax
+from jax.experimental import pallas as pl
+from jax.experimental.pallas import tpu as pltpu
 from jax.sharding import PartitionSpec as P
 
 
@@ -66,7 +70,7 @@
     return jnp.dot(left, right, precision=lax.Precision.HIGHEST, preferred_element_type=jnp.float32)
 
 
-def body(inverses, coupling, tile_mask, hess_diag):
+def direct_body(inverses, coupling, tile_mask, hess_diag):
     inverse = inverses[0]
     local = coupling[0]
     width = hess_diag.shape[0]
@@ -109,6 +113,511 @@
     return jnp.concatenate([lcol1, lcol2], axis=1)
 
 
+F32 = jnp.float32
+BF16 = jnp.bfloat16
+STEPS = 3
+SETTLED = 1.6e-5
+
+
+def split(x):
+    high = x.astype(BF16)
+    return high, (x - high.astype(F32)).astype(BF16)
+
+
+def dot(a, b, contract=((1,), (0,))):
+    return lax.dot_general(a, b, (contract, ((), ())), preferred_element_type=F32)
+
+
+def dot3(a, b, contract=((1,), (0,))):
+    (a_high, a_low), (b_high, b_low) = a, b
+    return (
+        dot(a_high, b_high, contract) + dot(a_high, b_low, contract) + dot(a_low, b_high, contract)
+    )
+
+
+NT = ((1,), (1,))
+
+
+def kernel(
+    n_scen,
+    n_col,
+    quarter,
+    sub,
+    inv_hbm,
+    coup_hbm,
+    mask_ref,
+    hess_ref,
+    out_ref,
+    flag_ref,
+    inv,
+    coup,
+    high_t,
+    low_t,
+    prod,
+    contrib,
+    slots,
+    corner_own,
+    corner_slots,
+    corner,
+    scaled_high,
+    scaled_low,
+    y,
+    y_next,
+    y_high,
+    y_low,
+    solve_in,
+    solve_out,
+    back,
+    load_sem,
+    ring_send,
+    ring_recv,
+    sum_send,
+    sum_recv,
+    corner_send,
+    corner_recv,
+    fill_send,
+    fill_recv,
+    in_send,
+    in_recv,
+    back_send,
+    back_recv,
+):
+    me = lax.axis_index("scen")
+    z = lax.axis_index("col")
+    depth = coup.shape[0]
+    block = coup.shape[1]
+    width = corner.shape[0]
+    chunk = prod.shape[2]
+    n_chunk = prod.shape[0]
+    rows = block // n_scen
+    piece = width // n_scen
+    owners = width // rows
+    tile = depth // mask_ref.shape[1]
+    half = depth // 2
+    n_sub = half // sub
+    nb = width // 2
+
+    barrier = pltpu.get_barrier_semaphore()
+
+    coup_panel = pltpu.make_async_copy(
+        coup_hbm.at[0, :, pl.ds(0, width)], coup.at[:, pl.ds(0, width)], load_sem.at[0]
+    )
+    coup_rest = pltpu.make_async_copy(
+        coup_hbm.at[0, :, pl.ds(width, block - width)],
+        coup.at[:, pl.ds(width, block - width)],
+        load_sem.at[1],
+    )
+    inv_load = pltpu.make_async_copy(inv_hbm.at[0], inv, load_sem.at[2])
+    coup_panel.start()
+
+    @pl.when(z == 0)
+    def _():
+        inv_load.start()
+
+    coup_rest.start()
+
+    def greet_scen(k, _):
+        pl.semaphore_signal(
+            barrier,
+            inc=1,
+            device_id={"scen": lax.rem(me + k, n_scen)},
+            device_id_type=pl.DeviceIdType.MESH,
+        )
+        return 0
+
+    def greet_col(k, _):
+        pl.semaphore_signal(
+            barrier,
+            inc=1,
+            device_id={"col": lax.rem(z + k, n_col)},
+            device_id_type=pl.DeviceIdType.MESH,
+        )
+        return 0
+
+    lax.fori_loop(1, n_scen, greet_scen, 0)
+    lax.fori_loop(1, n_col, greet_col, 0)
+    pl.semaphore_wait(barrier, n_scen + n_col - 2)
+
+    def ring_copy(q, way, s):
+        at = prod.at[q, pl.ds(pl.multiple_of(way * half + s * sub, sub), sub), :]
+        to = lax.rem(z + 1, n_col) if way == 0 else lax.rem(z + n_col - 1, n_col)
+        return pltpu.make_async_remote_copy(
+            src_ref=at,
+            dst_ref=at,
+            send_sem=ring_send.at[q, way, s],
+            recv_sem=ring_recv.at[q, way, s],
+            device_id={"col": to},
+            device_id_type=pl.DeviceIdType.MESH,
+        )
+
+    def transpose_coupling(first, count):
+        @pl.loop(0, depth // 128)
+        def _(t):
+            at = pl.ds(pl.multiple_of(t * 128, 128), 128)
+            high, low = split(coup[at, pl.ds(first, count)].T)
+            high_t[pl.ds(first, count), at] = high
+            low_t[pl.ds(first, count), at] = low
+
+    def contribute(q, first, count):
+        p = split(prod[q])
+
+        @pl.loop(0, count // quarter)
+        def _(r):
+            at = pl.ds(pl.multiple_of(first + r * quarter, quarter), quarter)
+            contrib[q, at, :] = dot3((high_t[at, :], low_t[at, :]), p)
+
+    def sum_copy(q, peer):
+        slot = lax.rem(me - peer + n_scen, n_scen) - 1
+        return pltpu.make_async_remote_copy(
+            src_ref=contrib.at[q, pl.ds(pl.multiple_of(peer * rows, rows), rows), :],
+            dst_ref=slots.at[q, slot],
+            send_sem=sum_send.at[q],
+            recv_sem=sum_recv.at[q],
+            device_id={"scen": peer},
+            device_id_type=pl.DeviceIdType.MESH,
+        )
+
+    def own_rows(q):
+        own = contrib[q, pl.ds(pl.multiple_of(me * rows, rows), rows), :]
+        return lax.fori_loop(0, n_scen - 1, lambda k, total: total + slots[q, k], own)
+
+    def in_copy(slot):
+        return pltpu.make_async_remote_copy(
+            src_ref=solve_in.at[slot],
+            dst_ref=solve_in.at[slot],
+            send_sem=in_send,
+            recv_sem=in_recv,
+            device_id={"col": 0},
+            device_id_type=pl.DeviceIdType.MESH,
+        )
+
+    def back_copy(to):
+        return pltpu.make_async_remote_copy(
+            src_ref=solve_out.at[to],
+            dst_ref=back,
+            send_sem=back_send,
+            recv_sem=back_recv,
+            device_id={"col": to},
+            device_id_type=pl.DeviceIdType.MESH,
+        )
+
+    @pl.when(z == 0)
+    def _():
+        coup_panel.wait()
+        transpose_coupling(0, width)
+        inv_load.wait()
+        keep = jnp.concatenate(
+            [
+                jnp.full((tile, 1), mask_ref[0, t], jnp.int32).astype(F32)
+                for t in range(mask_ref.shape[1])
+            ],
+            axis=0,
+        )
+
+        for q in range(n_chunk):
+            panel = split(coup[:, pl.ds(q * chunk, chunk)] * keep)
+            for r in range(depth // quarter):
+                n_half = half // quarter
+                r = (r % 2) * n_half + r // 2
+                kept = inv[pl.ds(r * quarter, quarter), :]
+                scale = keep[r * quarter : (r + 1) * quarter]
+                prod[q, pl.ds(r * quarter, quarter), :] = dot3(split(kept), panel) * scale
+                way = r // n_half
+                for s in range(quarter // sub):
+                    ring_copy(q, way, (r % n_half) * (quarter // sub) + s).start()
+
+        for q in range(n_chunk):
+            p = split(prod[q])
+            for r in range(width // quarter):
+                at = pl.ds(r * quarter, quarter)
+                corner_own[at, pl.ds(q * chunk, chunk)] = dot3((high_t[at, :], low_t[at, :]), p)
+
+        def corner_start(k, _):
+            peer = lax.rem(me + k, n_scen)
+            pltpu.make_async_remote_copy(
+                src_ref=corner_own.at[pl.ds(pl.multiple_of(peer * piece, piece), piece), :],
+                dst_ref=corner_slots.at[n_scen - 1 - k],
+                send_sem=corner_send,
+                recv_sem=corner_recv,
+                device_id={"scen": peer},
+                device_id_type=pl.DeviceIdType.MESH,
+            ).start()
+            return 0
+
+        lax.fori_loop(1, n_scen, corner_start, 0)
+
+        coup_rest.wait()
+        transpose_coupling(width, block - width)
+        for q in range(n_chunk):
+            contribute(q, width, block - width)
+
+        mine = pl.ds(pl.multiple_of(me * piece, piece), piece)
+        pltpu.make_async_copy(corner_slots, corner_slots, corner_recv).wait()
+        total = lax.fori_loop(
+            0, n_scen - 1, lambda k, total: total + corner_slots[k], corner_own[mine, :]
+        )
+        row = me * piece + lax.broadcasted_iota(jnp.int32, (piece, width), 0)
+        column = lax.broadcasted_iota(jnp.int32, (piece, width), 1)
+        corner[mine, :] = total + jnp.where(row == column, hess_ref[...], 0.0)
+
+        def fill_copy(k):
+            return pltpu.make_async_remote_copy(
+                src_ref=corner.at[mine, :],
+                dst_ref=corner.at[mine, :],
+                send_sem=fill_send,
+                recv_sem=fill_recv.at[n_scen - 1 - k],
+                device_id={"scen": lax.rem(me + k, n_scen)},
+                device_id_type=pl.DeviceIdType.MESH,
+            )
+
+        def fill_start(k, _):
+            fill_copy(k).start()
+            return 0
+
+        lax.fori_loop(1, n_scen, fill_start, 0)
+
+        def sum_start(k, _):
+            peer = lax.rem(me + k, n_scen)
+
+            @pl.when(peer >= owners)
+            def _():
+                for q in range(n_chunk):
+                    sum_copy(q, peer).start()
+
+            return 0
+
+        lax.fori_loop(1, n_scen, sum_start, 0)
+
+        def fill_wait(k, _):
+            from_peer = lax.rem(me + k, n_scen)
+            theirs = corner.at[pl.ds(pl.multiple_of(from_peer * piece, piece), piece), :]
+            pltpu.make_async_copy(theirs, theirs, fill_recv.at[k - 1]).wait()
+            return 0
+
+        lax.fori_loop(1, n_scen, fill_wait, 0)
+
+        row = lax.broadcasted_iota(jnp.int32, (width, width), 0)
+        column = lax.broadcasted_iota(jnp.int32, (width, width), 1)
+        on_diagonal = jnp.where(row == column, corner[...], 0.0)
+        root_row = lax.rsqrt(jnp.sum(on_diagonal, axis=0, keepdims=True))
+        root_column = lax.rsqrt(jnp.sum(on_diagonal, axis=1, keepdims=True))
+        scaled = corner[...] * root_column * root_row
+        high, low = split(scaled)
+        scaled_high[...] = high
+        scaled_low[...] = low
+        y[...] = jnp.where(row == column, 1.0, jnp.where(row > column, -scaled, 0.0))
+
+        for step in range(STEPS):
+            high, low = split(y[...])
+            y_high[...] = high
+            y_low[...] = low
+            size = jnp.zeros((1, 1), F32)
+            for r in range(2):
+                at = pl.ds(r * nb, nb)
+                to = pl.ds(0, (r + 1) * nb)
+                t = dot3((y_high[at, to], y_low[at, to]), (scaled_high[to, to], scaled_low[to, to]))
+                e = dot3(split(t), (y_high[to, to], y_low[to, to]), NT)
+                e_row = r * nb + lax.broadcasted_iota(jnp.int32, e.shape, 0)
+                e_column = lax.broadcasted_iota(jnp.int32, e.shape, 1)
+                e = jnp.where(e_row == e_column, e - 1.0, jnp.where(e_row > e_column, e, 0.0))
+                if step == STEPS - 1:
+                    size = size + jnp.sum(e * e, keepdims=True)
+                e = jnp.where(e_row == e_column, 0.5 * e, e)
+                y_next[at, to] = y[at, to] - dot3(split(e), (y_high[to, to], y_low[to, to]))
+            for r in range(2):
+                at = pl.ds(r * nb, nb)
+                to = pl.ds(0, (r + 1) * nb)
+                y[at, to] = y_next[at, to]
+
+        bad = jnp.where(size < SETTLED, 0.0, 1.0)
+        y_final = split(y[...])
+
+        @pl.when(me < owners)
+        def _():
+            solve_in[0] = corner[
+                pl.ds(pl.multiple_of(lax.rem(me, owners) * rows, rows), rows), :
+            ]
+
+        @pl.when(me >= owners)
+        def _():
+            for q in range(n_chunk):
+                pltpu.make_async_copy(slots.at[q], slots.at[q], sum_recv.at[q]).wait()
+                solve_in[0, :, pl.ds(q * chunk, chunk)] = own_rows(q)
+
+        rest = solve_in.at[pl.ds(1, n_col - 1)]
+        pltpu.make_async_copy(rest, rest, in_recv).wait()
+        given = solve_in[...].reshape(n_col * rows, width) * root_row
+        solved = dot3(split(given), y_final, NT).reshape(n_col, rows, width)
+        solve_out[:, pl.ds(0, rows), :] = solved
+        solve_out[:, pl.ds(rows, 8), :] = jnp.broadcast_to(bad, (n_col, 8, width))
+
+        def back_start(k, _):
+            back_copy(k).start()
+            return 0
+
+        lax.fori_loop(1, n_col, back_start, 0)
+        row = me * rows + lax.broadcasted_iota(jnp.int32, (rows, width), 0)
+        column = lax.broadcasted_iota(jnp.int32, (rows, width), 1)
+        out_ref[...] = jnp.where(column <= row, solved[0], 0.0)
+        flag_ref[...] = jnp.broadcast_to(bad, flag_ref.shape)
+
+        for q in range(n_chunk):
+            for way in range(2):
+                for s in range(n_sub):
+                    ring_copy(q, way, s).wait_send()
+        pltpu.make_async_copy(corner_slots, corner_slots, corner_send).wait()
+        pltpu.make_async_copy(corner_slots, corner_slots, fill_send).wait()
+        for q in range(n_chunk):
+
+            @pl.when(me < owners)
+            def _():
+                some = slots.at[q, pl.ds(0, n_scen - owners)]
+                pltpu.make_async_copy(some, some, sum_send.at[q]).wait()
+
+            @pl.when(me >= owners)
+            def _():
+                some = slots.at[q, pl.ds(0, n_scen - owners - 1)]
+                pltpu.make_async_copy(some, some, sum_send.at[q]).wait()
+
+        some = solve_out.at[pl.ds(1, n_col - 1)]
+        pltpu.make_async_copy(some, some, back_send).wait()
+
+    @pl.when(z != 0)
+    def _():
+        coup_panel.wait()
+        coup_rest.wait()
+        transpose_coupling(0, block)
+
+        def sum_start(q):
+            def start(k, _):
+                sum_copy(q, lax.rem(me + k, n_scen)).start()
+                return 0
+
+            lax.fori_loop(1, n_scen, start, 0)
+
+        for q in range(n_chunk):
+
+            @pl.loop(0, n_sub)
+            def _(s):
+                up = ring_copy(q, 0, s)
+                up.wait_recv()
+
+                @pl.when(z < n_col - 1)
+                def _():
+                    up.start()
+
+                down = ring_copy(q, 1, s)
+                down.wait_recv()
+
+                @pl.when(z > 1)
+                def _():
+                    down.start()
+
+            contribute(q, 0, block)
+            sum_start(q)
+
+        for q in range(n_chunk):
+            pltpu.make_async_copy(slots.at[q], slots.at[q], sum_recv.at[q]).wait()
+            solve_in[z, :, pl.ds(q * chunk, chunk)] = own_rows(q)
+        in_copy(z).start()
+
+        for q in range(n_chunk):
+
+            @pl.loop(0, n_sub)
+            def _(s):
+                @pl.when(z < n_col - 1)
+                def _():
+                    ring_copy(q, 0, s).wait_send()
+
+                @pl.when(z > 1)
+                def _():
+                    ring_copy(q, 1, s).wait_send()
+
+            pltpu.make_async_copy(slots.at[q], slots.at[q], sum_send.at[q]).wait()
+        in_copy(z).wait_send()
+        pltpu.make_async_copy(back, back, back_recv).wait()
+        out_ref[...] = back[pl.ds(0, rows), :]
+        flag_ref[...] = back[pl.ds(rows, 8), pl.ds(0, 128)]
+
+
+def fused(inverses, coupling, tile_mask, hess_diag, quarter=256, chunk=256, sub=64):
+    n_scen = lax.axis_size("scen")
+    n_col = lax.axis_size("col")
+    _, depth, block = coupling.shape
+    width = hess_diag.shape[0]
+    rows = block // n_scen
+    piece = width // n_scen
+    n_chunk = width // chunk
+    n_sub = depth // 2 // sub
+    vmem = pltpu.VMEM
+    dma = pltpu.SemaphoreType.DMA
+    scratch = [
+        vmem((depth, depth), F32),
+        vmem((depth, block), F32),
+        vmem((block, depth), BF16),
+        vmem((block, depth), BF16),
+        vmem((n_chunk, depth, chunk), F32),
+        vmem((n_chunk, block, chunk), F32),
+        vmem((n_chunk, n_scen - 1, rows, chunk), F32),
+        vmem((width, width), F32),
+        vmem((n_scen - 1, piece, width), F32),
+        vmem((width, width), F32),
+        vmem((width, width), BF16),
+        vmem((width, width), BF16),
+        vmem((width, width), F32),
+        vmem((width, width), F32),
+        vmem((width, width), BF16),
+        vmem((width, width), BF16),
+        vmem((n_col, rows, width), F32),
+        vmem((n_col, rows + 8, width), F32),
+        vmem((rows + 8, width), F32),
+        dma((3,)),
+        dma((n_chunk, 2, n_sub)),
+        dma((n_chunk, 2, n_sub)),
+        dma((n_chunk,)),
+        dma((n_chunk,)),
+        dma(()),
+        dma(()),
+        dma(()),
+        dma((n_scen - 1,)),
+        dma(()),
+        dma(()),
+        dma(()),
+        dma(()),
+    ]
+    return pl.pallas_call(
+        functools.partial(kernel, n_scen, n_col, quarter, sub),
+        out_shape=(
+            jax.ShapeDtypeStruct((rows, width), F32),
+            jax.ShapeDtypeStruct((8, 128), F32),
+        ),
+        in_specs=[
+            pl.BlockSpec(memory_space=pl.ANY),
+            pl.BlockSpec(memory_space=pl.ANY),
+            pl.BlockSpec(memory_space=pltpu.SMEM),
+            pl.BlockSpec(memory_space=pltpu.VMEM),
+        ],
+        out_specs=[pl.BlockSpec(memory_space=pltpu.VMEM)] * 2,
+        scratch_shapes=scratch,
+        compiler_params=pltpu.CompilerParams(
+            collective_id=0, has_side_effects=True, vmem_limit_bytes=50 * 2**20
+        ),
+    )(inverses, coupling, tile_mask, hess_diag[None, :])
+
+
+def body(inverses, coupling, tile_mask, hess_diag):
+    factor, flag = fused(inverses, coupling, tile_mask, hess_diag)
+    return lax.cond(
+        flag[0, 0] > 0.5,
+        direct_body,
+        lambda *_: factor,
+        inverses,
+        coupling,
+        tile_mask,
+        hess_diag,
+    )
+
+
 def solution(mesh):
     in_specs = (P("scen", None, None), P("scen", None, "col"), P("scen", None), P())
     out_specs = P(("col", "scen"), None)

time: 452 us -> 705 us (1.56)
  Pallas kernels: 0 us -> 689 us
  waiting for transfers between devices: 203 us -> 0 us
  other arithmetic: 113 us -> 0 us
  blocking collectives: 55.5 us -> 0 us
  matrix products: 30 us -> 0 us
  local copies, waits for them, and re-layouts: 18.7 us -> 1.15 us
  starting transfers between devices: 7.7 us -> 0 us
    pallas_call x0 -> x1, Pallas kernels: none -> 689 us  [fused(): pl.pallas_call(functools.partial(kernel, n_scen, n_col, quarter, sub), ou...]
    all_gather x3 -> x0, waiting for transfers between devices: 132 us -> none  [the longest x2 90.6 us: from_root(): lax.all_gather(x, axis)]
    another operation x19 -> x0, other arithmetic: 108 us -> none  [the longest x7 34.7 us: body(): chol2 = jnp.linalg.cholesky(update)]
    all_to_all x2 -> x0, blocking collectives: 55.5 us -> none  [sent_to_all(): lax.all_to_all(jnp.broadcast_to(x[None], (size, *x.shape)), axis, 0, 0, t...]
    reduce_scatter x1 -> x0, waiting for transfers between devices: 45.4 us -> none  [spread(): own = lax.psum_scatter(padded, axis, scatter_dimension=0, tiled=True)]
    dot_general x6 -> x0, matrix products: 27.3 us -> none  [the longest x5 20.4 us: matmul(): jnp.dot(left, right, precision=lax.Precision.HIGHEST, preferred_element_t...]
    all_to_all x1 -> x0, waiting for transfers between devices: 25.5 us -> none  [sum_at_owner(): blocks = lax.all_to_all(in_blocks(x, dim, size), axis, 0, 0, tiled=True)]
    another operation x20 -> x0, local copies, waits for them, and re-layouts: 8.05 us -> none  [the longest x9 4.04 us: body(): inv1 = jax.scipy.linalg.solve_triangular(chol1, identity, lower=True)]
  transfers between devices with their start and end apart: 5 -> 0, of which waited for: 5 -> 0; matrix products, arithmetic and copies ran while one was open for 0% -> 0% of each run, Pallas kernels for 0% -> 0%
where the time goes in v1:
time: 705 us
  Pallas kernels  689 us (98%)
  between operations  14.1 us (2%)
    pallas_call x1, Pallas kernels, fused(): pl.pallas_call(functools.partial(kernel, n_scen, n_col, quarter, sub), ou...  689 us

profile of v1, /device:TPU:6, one launch (start us, length us, event | category | flops | bytes accessed | tf_op | source)
XLA Modules:
  0.0 704.8 jit_solution(7788750863917743450)
XLA Ops:
  6.5 0.0 copy-start.1
  6.5 0.0 copy-start.2
  6.5 689.2 %shard_map.48 = (f32[32,512]{1,0:T(8,128)S(1)}, f32[8,128]{1,0:T(8,128)S(1)}) custom-call(f32[1,1024,1024]{2,1,0:T(8,128)} %inv_hbm.1, f32[1,1024,1024]{2,1,0:T(8,128)} %coup_hbm.1, s32[1,8]{1,0:T(1,128)} %mask_ref.1, f32[1,512]{1,0:T(1,128)} %bitcast.106), custom_call_target="tpu_custom_call" | custom-call | tf_op jit(solution)/shard_map/pallas_call | solution.py:588
  695.8 0.5 slice.65
  697.0 0.0 copy-done.1
  697.0 0.0 copy-done.2
  697.0 0.3 conditional.1
  697.3 0.6 copy.53
Async XLA Ops:
  6.5 690.4 %copy-start.1 = (f32[512]{0:T(512)S(1)}, f32[512]{0:T(512)}, u32[]{:S(2)}) copy-start(f32[512]{0:T(512)} %param.12) | copy-start | bytes 6148
  6.5 690.4 %copy-start.2 = (s32[1,8]{1,0:T(1,128)S(1)}, s32[1,8]{1,0:T(1,128)}, u32[]{:S(2)}) copy-start(s32[1,8]{1,0:T(1,128)} %mask_ref.1) | copy-start | bytes 100

commit v2 on v1

--- a/solution.py
+++ b/solution.py
@@ -154,6 +154,8 @@
     high_t,
     low_t,
     prod,
+    prod_high,
+    prod_low,
     contrib,
     slots,
     corner_own,
@@ -238,14 +240,15 @@
     lax.fori_loop(1, n_col, greet_col, 0)
     pl.semaphore_wait(barrier, n_scen + n_col - 2)
 
-    def ring_copy(q, way, s):
-        at = prod.at[q, pl.ds(pl.multiple_of(way * half + s * sub, sub), sub), :]
+    def ring_copy(way, g):
+        s = lax.rem(g, n_sub)
+        at = prod.at[g // n_sub, pl.ds(pl.multiple_of(way * half + s * sub, sub), sub), :]
         to = lax.rem(z + 1, n_col) if way == 0 else lax.rem(z + n_col - 1, n_col)
         return pltpu.make_async_remote_copy(
             src_ref=at,
             dst_ref=at,
-            send_sem=ring_send.at[q, way, s],
-            recv_sem=ring_recv.at[q, way, s],
+            send_sem=ring_send.at[way, g],
+            recv_sem=ring_recv.at[way, g],
             device_id={"col": to},
             device_id_type=pl.DeviceIdType.MESH,
         )
@@ -258,13 +261,16 @@
             high_t[pl.ds(first, count), at] = high
             low_t[pl.ds(first, count), at] = low
 
-    def contribute(q, first, count):
-        p = split(prod[q])
-
-        @pl.loop(0, count // quarter)
-        def _(r):
-            at = pl.ds(pl.multiple_of(first + r * quarter, quarter), quarter)
-            contrib[q, at, :] = dot3((high_t[at, :], low_t[at, :]), p)
+    def split_prod(q):
+        high, low = split(prod[q])
+        prod_high[...] = high
+        prod_low[...] = low
+
+    def contribute(q, first):
+        at = pl.ds(pl.multiple_of(first, quarter), quarter)
+        contrib[q, at, :] = dot3(
+            (high_t[at, :], low_t[at, :]), (prod_high[...], prod_low[...])
+        )
 
     def sum_copy(q, peer):
         slot = lax.rem(me - peer + n_scen, n_scen) - 1
@@ -324,7 +330,7 @@
                 prod[q, pl.ds(r * quarter, quarter), :] = dot3(split(kept), panel) * scale
                 way = r // n_half
                 for s in range(quarter // sub):
-                    ring_copy(q, way, (r % n_half) * (quarter // sub) + s).start()
+                    ring_copy(way, q * n_sub + (r % n_half) * (quarter // sub) + s).start()
 
         for q in range(n_chunk):
             p = split(prod[q])
@@ -349,7 +355,12 @@
         coup_rest.wait()
         transpose_coupling(width, block - width)
         for q in range(n_chunk):
-            contribute(q, width, block - width)
+            split_prod(q)
+
+            @pl.loop(width // quarter, block // quarter)
+            def _(r):
+                contribute(q, r * quarter)
+
 
         mine = pl.ds(pl.multiple_of(me * piece, piece), piece)
         pltpu.make_async_copy(corner_slots, corner_slots, corner_recv).wait()
@@ -461,10 +472,11 @@
         out_ref[...] = jnp.where(column <= row, solved[0], 0.0)
         flag_ref[...] = jnp.broadcast_to(bad, flag_ref.shape)
 
-        for q in range(n_chunk):
-            for way in range(2):
-                for s in range(n_sub):
-                    ring_copy(q, way, s).wait_send()
+        @pl.loop(0, n_chunk * n_sub)
+        def _(g):
+            ring_copy(0, g).wait_send()
+            ring_copy(1, g).wait_send()
+
         pltpu.make_async_copy(corner_slots, corner_slots, corner_send).wait()
         pltpu.make_async_copy(corner_slots, corner_slots, fill_send).wait()
         for q in range(n_chunk):
@@ -488,33 +500,65 @@
         coup_rest.wait()
         transpose_coupling(0, block)
 
-        def sum_start(q):
+        def form(q, r):
+            contribute(q, r * quarter)
+            per = quarter // rows
+
             def start(k, _):
-                sum_copy(q, lax.rem(me + k, n_scen)).start()
+                peer = lax.rem(me + k, per) + r * per
+
+                @pl.when(peer != me)
+                def _():
+                    sum_copy(q, peer).start()
+
                 return 0
 
-            lax.fori_loop(1, n_scen, start, 0)
-
-        for q in range(n_chunk):
-
-            @pl.loop(0, n_sub)
-            def _(s):
-                up = ring_copy(q, 0, s)
+            lax.fori_loop(0, per, start, 0)
+
+        late = jnp.maximum(z - 1, n_col - 1 - z)
+        n_piece = n_chunk * n_sub
+        n_row = block // quarter
+
+        @pl.loop(0, n_piece + late)
+        def _(t):
+            g = t - (z - 1)
+
+            @pl.when(jnp.logical_and(g >= 0, g < n_piece))
+            def _():
+                up = ring_copy(0, g)
                 up.wait_recv()
 
                 @pl.when(z < n_col - 1)
                 def _():
                     up.start()
 
-                down = ring_copy(q, 1, s)
+            h = t - (n_col - 1 - z)
+
+            @pl.when(jnp.logical_and(h >= 0, h < n_piece))
+            def _():
+                down = ring_copy(1, h)
                 down.wait_recv()
 
                 @pl.when(z > 1)
                 def _():
                     down.start()
 
-            contribute(q, 0, block)
-            sum_start(q)
+            done = t - late + 1
+            q = done // n_sub - 1
+            r = lax.rem(done, n_sub)
+            whole = done >= n_sub
+
+            @pl.when(jnp.logical_and(whole, r == 0))
+            def _():
+                split_prod(q)
+
+            @pl.when(jnp.logical_and(jnp.logical_and(whole, r < n_row), done < n_piece))
+            def _():
+                form(q, r)
+
+        @pl.loop(0, n_row)
+        def _(r):
+            form(n_chunk - 1, r)
 
         for q in range(n_chunk):
             pltpu.make_async_copy(slots.at[q], slots.at[q], sum_recv.at[q]).wait()
@@ -523,24 +567,25 @@
 
         for q in range(n_chunk):
 
-            @pl.loop(0, n_sub)
-            def _(s):
-                @pl.when(z < n_col - 1)
-                def _():
-                    ring_copy(q, 0, s).wait_send()
-
-                @pl.when(z > 1)
-                def _():
-                    ring_copy(q, 1, s).wait_send()
-
             pltpu.make_async_copy(slots.at[q], slots.at[q], sum_send.at[q]).wait()
         in_copy(z).wait_send()
+
+        @pl.loop(0, n_piece)
+        def _(g):
+            @pl.when(z < n_col - 1)
+            def _():
+                ring_copy(0, g).wait_send()
+
+            @pl.when(z > 1)
+            def _():
+                ring_copy(1, g).wait_send()
+
         pltpu.make_async_copy(back, back, back_recv).wait()
         out_ref[...] = back[pl.ds(0, rows), :]
         flag_ref[...] = back[pl.ds(rows, 8), pl.ds(0, 128)]
 
 
-def fused(inverses, coupling, tile_mask, hess_diag, quarter=256, chunk=256, sub=64):
+def fused(inverses, coupling, tile_mask, hess_diag, quarter=256, chunk=256, sub=128):
     n_scen = lax.axis_size("scen")
     n_col = lax.axis_size("col")
     _, depth, block = coupling.shape
@@ -557,6 +602,8 @@
         vmem((block, depth), BF16),
         vmem((block, depth), BF16),
         vmem((n_chunk, depth, chunk), F32),
+        vmem((depth, chunk), BF16),
+        vmem((depth, chunk), BF16),
         vmem((n_chunk, block, chunk), F32),
         vmem((n_chunk, n_scen - 1, rows, chunk), F32),
         vmem((width, width), F32),
@@ -572,8 +619,8 @@
         vmem((n_col, rows + 8, width), F32),
         vmem((rows + 8, width), F32),
         dma((3,)),
-        dma((n_chunk, 2, n_sub)),
-        dma((n_chunk, 2, n_sub)),
+        dma((2, n_chunk * n_sub)),
+        dma((2, n_chunk * n_sub)),
         dma((n_chunk,)),
         dma((n_chunk,)),
         dma(()),

time: 705 us -> 116 us (0.16)
  Pallas kernels: 689 us -> 98.6 us
    pallas_call x1, Pallas kernels: 689 us -> 98.6 us  [fused(): pl.pallas_call(functools.partial(kernel, n_scen, n_col, quarter, sub), ou...]
where the time goes in v2:
time: 116 us; the launch traced here: 114 us
  Pallas kernels  98.6 us (85%)
  between operations  14.1 us (12%)
    pallas_call x1, Pallas kernels, fused(): pl.pallas_call(functools.partial(kernel, n_scen, n_col, quarter, sub), ou...  98.6 us

profile of v2, /device:TPU:6, one launch (start us, length us, event | category | flops | bytes accessed | tf_op | source)
XLA Modules:
  0.0 114.1 jit_solution(15373483691003950164)
XLA Ops:
  6.5 0.0 copy-start.1
  6.5 0.0 copy-start.2
  6.5 98.6 %shard_map.48 = (f32[32,512]{1,0:T(8,128)S(1)}, f32[8,128]{1,0:T(8,128)S(1)}) custom-call(f32[1,1024,1024]{2,1,0:T(8,128)} %inv_hbm.1, f32[1,1024,1024]{2,1,0:T(8,128)} %coup_hbm.1, s32[1,8]{1,0:T(1,128)} %mask_ref.1, f32[1,512]{1,0:T(1,128)} %bitcast.106), custom_call_target="tpu_custom_call" | custom-call | tf_op jit(solution)/shard_map/pallas_call | solution.py:635
  105.1 0.5 slice.65
  106.3 0.0 copy-done.1
  106.3 0.0 copy-done.2
  106.3 0.3 conditional.1
  106.6 0.6 copy.53
Async XLA Ops:
  6.5 99.8 %copy-start.1 = (f32[512]{0:T(512)S(1)}, f32[512]{0:T(512)}, u32[]{:S(2)}) copy-start(f32[512]{0:T(512)} %param.12) | copy-start | bytes 6148
  6.5 99.8 %copy-start.2 = (s32[1,8]{1,0:T(1,128)S(1)}, s32[1,8]{1,0:T(1,128)}, u32[]{:S(2)}) copy-start(s32[1,8]{1,0:T(1,128)} %mask_ref.1) | copy-start | bytes 100

commit v3 on v2

--- a/solution.py
+++ b/solution.py
@@ -143,6 +143,7 @@
     n_col,
     quarter,
     sub,
+    lag,
     inv_hbm,
     coup_hbm,
     mask_ref,
@@ -157,9 +158,11 @@
     prod_high,
     prod_low,
     contrib,
+    pair_slots,
     slots,
-    corner_own,
-    corner_slots,
+    plane_own,
+    plane_pair,
+    plane_slots,
     corner,
     scaled_high,
     scaled_low,
@@ -170,25 +173,34 @@
     solve_in,
     solve_out,
     back,
+    late_out,
     load_sem,
     ring_send,
     ring_recv,
+    pair_send,
+    pair_recv,
     sum_send,
     sum_recv,
-    corner_send,
-    corner_recv,
+    plane_pair_send,
+    plane_pair_recv,
+    plane_send,
+    plane_recv,
     fill_send,
     fill_recv,
+    fill_pair_send,
+    fill_pair_recv,
     in_send,
     in_recv,
     back_send,
     back_recv,
+    late_send,
+    late_recv,
 ):
     me = lax.axis_index("scen")
     z = lax.axis_index("col")
     depth = coup.shape[0]
     block = coup.shape[1]
-    width = corner.shape[0]
+    width = corner.shape[3]
     chunk = prod.shape[2]
     n_chunk = prod.shape[0]
     rows = block // n_scen
@@ -198,6 +210,11 @@
     half = depth // 2
     n_sub = half // sub
     nb = width // 2
+    n_chip = n_scen // 2
+    chip = me // 2
+    core = lax.rem(me, 2)
+    other = 1 - core
+    partner = chip * 2 + other
 
     barrier = pltpu.get_barrier_semaphore()
 
@@ -266,26 +283,51 @@
         prod_high[...] = high
         prod_low[...] = low
 
-    def contribute(q, first):
-        at = pl.ds(pl.multiple_of(first, quarter), quarter)
-        contrib[q, at, :] = dot3(
-            (high_t[at, :], low_t[at, :]), (prod_high[...], prod_low[...])
-        )
-
-    def sum_copy(q, peer):
-        slot = lax.rem(me - peer + n_scen, n_scen) - 1
+    per = quarter // rows // 2
+
+    def pair_copy(q, r):
+        at = pl.ds(pl.multiple_of(r * per, per), per)
         return pltpu.make_async_remote_copy(
-            src_ref=contrib.at[q, pl.ds(pl.multiple_of(peer * rows, rows), rows), :],
-            dst_ref=slots.at[q, slot],
-            send_sem=sum_send.at[q],
-            recv_sem=sum_recv.at[q],
-            device_id={"scen": peer},
+            src_ref=contrib.at[q, at, other],
+            dst_ref=pair_slots.at[q, at],
+            send_sem=pair_send.at[q],
+            recv_sem=pair_recv.at[q, r],
+            device_id={"scen": partner},
             device_id_type=pl.DeviceIdType.MESH,
         )
 
+    def form(q, r):
+        at = pl.ds(pl.multiple_of(r * quarter, quarter), quarter)
+        term = dot3((high_t[at, :], low_t[at, :]), (prod_high[...], prod_low[...]))
+        contrib[q, pl.ds(pl.multiple_of(r * per, per), per)] = term.reshape(per, 2, rows, chunk)
+        pair_copy(q, r).start()
+
+    def pass_on(q, r):
+        pair_copy(q, r).wait_recv()
+        at = pl.ds(pl.multiple_of(r * per, per), per)
+        contrib[q, at, core] = contrib[q, at, core] + pair_slots[q, at]
+
+        def start(k, _):
+            to = lax.rem(chip + k, per) + r * per
+
+            @pl.when(to != chip)
+            def _():
+                pltpu.make_async_remote_copy(
+                    src_ref=contrib.at[q, to, core],
+                    dst_ref=slots.at[q, lax.rem(chip - to + n_chip, n_chip) - 1],
+                    send_sem=sum_send.at[q],
+                    recv_sem=sum_recv.at[q],
+                    device_id={"scen": to * 2 + core},
+                    device_id_type=pl.DeviceIdType.MESH,
+                ).start()
+
+            return 0
+
+        lax.fori_loop(0, per, start, 0)
+
     def own_rows(q):
-        own = contrib[q, pl.ds(pl.multiple_of(me * rows, rows), rows), :]
-        return lax.fori_loop(0, n_scen - 1, lambda k, total: total + slots[q, k], own)
+        own = contrib[q, chip, core]
+        return lax.fori_loop(0, n_chip - 1, lambda k, total: total + slots[q, k], own)
 
     def in_copy(slot):
         return pltpu.make_async_remote_copy(
@@ -332,52 +374,87 @@
                 for s in range(quarter // sub):
                     ring_copy(way, q * n_sub + (r % n_half) * (quarter // sub) + s).start()
 
-        for q in range(n_chunk):
-            p = split(prod[q])
-            for r in range(width // quarter):
-                at = pl.ds(r * quarter, quarter)
-                corner_own[at, pl.ds(q * chunk, chunk)] = dot3((high_t[at, :], low_t[at, :]), p)
-
-        def corner_start(k, _):
-            peer = lax.rem(me + k, n_scen)
-            pltpu.make_async_remote_copy(
-                src_ref=corner_own.at[pl.ds(pl.multiple_of(peer * piece, piece), piece), :],
-                dst_ref=corner_slots.at[n_scen - 1 - k],
-                send_sem=corner_send,
-                recv_sem=corner_recv,
-                device_id={"scen": peer},
+        def plane_pair_copy(part):
+            return pltpu.make_async_remote_copy(
+                src_ref=plane_own.at[part, :, other],
+                dst_ref=plane_pair.at[part],
+                send_sem=plane_pair_send.at[part],
+                recv_sem=plane_pair_recv.at[part],
+                device_id={"scen": partner},
                 device_id_type=pl.DeviceIdType.MESH,
-            ).start()
-            return 0
-
-        lax.fori_loop(1, n_scen, corner_start, 0)
-
+            )
+
+        def plane_form(part):
+            group = quarter // piece // 2
+            for q in range(n_chunk):
+                split_prod(q)
+                for r in range(width // quarter):
+                    at = pl.ds(part * width + r * quarter, quarter)
+                    term = dot3((high_t[at, :], low_t[at, :]), (prod_high[...], prod_low[...]))
+                    plane_own[part, pl.ds(r * group, group), :, :, pl.ds(q * chunk, chunk)] = (
+                        term.reshape(group, 2, piece, chunk)
+                    )
+            plane_pair_copy(part).start()
+
+        def plane_pass_on(part):
+            plane_pair_copy(part).wait_recv()
+            step = max(1, n_chip // 4)
+            for r in range(0, n_chip, step):
+                at = pl.ds(r, step)
+                plane_own[part, at, core] = plane_own[part, at, core] + plane_pair[part, at]
+
+            def start(k, _):
+                to = lax.rem(chip + k, n_chip)
+                pltpu.make_async_remote_copy(
+                    src_ref=plane_own.at[part, to, core],
+                    dst_ref=plane_slots.at[part, n_chip - 1 - k],
+                    send_sem=plane_send.at[part],
+                    recv_sem=plane_recv.at[part],
+                    device_id={"scen": to * 2 + core},
+                    device_id_type=pl.DeviceIdType.MESH,
+                ).start()
+                return 0
+
+            lax.fori_loop(1, n_chip, start, 0)
+
+        def plane_total(part):
+            some = plane_slots.at[part]
+            pltpu.make_async_copy(some, some, plane_recv.at[part]).wait()
+            return lax.fori_loop(
+                0,
+                n_chip - 1,
+                lambda k, total: total + plane_slots[part, k],
+                plane_own[part, chip, core],
+            )
+
+        plane_form(0)
         coup_rest.wait()
         transpose_coupling(width, block - width)
-        for q in range(n_chunk):
-            split_prod(q)
-
-            @pl.loop(width // quarter, block // quarter)
-            def _(r):
-                contribute(q, r * quarter)
-
-
-        mine = pl.ds(pl.multiple_of(me * piece, piece), piece)
-        pltpu.make_async_copy(corner_slots, corner_slots, corner_recv).wait()
-        total = lax.fori_loop(
-            0, n_scen - 1, lambda k, total: total + corner_slots[k], corner_own[mine, :]
-        )
+        plane_pass_on(0)
+        plane_form(1)
+        total = plane_total(0)
         row = me * piece + lax.broadcasted_iota(jnp.int32, (piece, width), 0)
         column = lax.broadcasted_iota(jnp.int32, (piece, width), 1)
-        corner[mine, :] = total + jnp.where(row == column, hess_ref[...], 0.0)
+        corner[chip, core] = total + jnp.where(row == column, hess_ref[...], 0.0)
 
         def fill_copy(k):
             return pltpu.make_async_remote_copy(
-                src_ref=corner.at[mine, :],
-                dst_ref=corner.at[mine, :],
+                src_ref=corner.at[chip, core],
+                dst_ref=corner.at[chip, core],
                 send_sem=fill_send,
-                recv_sem=fill_recv.at[n_scen - 1 - k],
-                device_id={"scen": lax.rem(me + k, n_scen)},
+                recv_sem=fill_recv.at[n_chip - 1 - k],
+                device_id={"scen": lax.rem(chip + k, n_chip) * 2 + core},
+                device_id_type=pl.DeviceIdType.MESH,
+            )
+
+        def hand_copy(k, which):
+            at = corner.at[lax.rem(chip + k, n_chip), which]
+            return pltpu.make_async_remote_copy(
+                src_ref=at,
+                dst_ref=at,
+                send_sem=fill_pair_send,
+                recv_sem=fill_pair_recv.at[k],
+                device_id={"scen": partner},
                 device_id_type=pl.DeviceIdType.MESH,
             )
 
@@ -385,34 +462,31 @@
             fill_copy(k).start()
             return 0
 
-        lax.fori_loop(1, n_scen, fill_start, 0)
-
-        def sum_start(k, _):
-            peer = lax.rem(me + k, n_scen)
-
-            @pl.when(peer >= owners)
-            def _():
-                for q in range(n_chunk):
-                    sum_copy(q, peer).start()
-
+        hand_copy(0, core).start()
+        lax.fori_loop(1, n_chip, fill_start, 0)
+
+        def fill_hand(k, _):
+            theirs = corner.at[lax.rem(chip + k, n_chip), core]
+            pltpu.make_async_copy(theirs, theirs, fill_recv.at[k - 1]).wait()
+            hand_copy(k, core).start()
             return 0
 
-        lax.fori_loop(1, n_scen, sum_start, 0)
-
-        def fill_wait(k, _):
-            from_peer = lax.rem(me + k, n_scen)
-            theirs = corner.at[pl.ds(pl.multiple_of(from_peer * piece, piece), piece), :]
-            pltpu.make_async_copy(theirs, theirs, fill_recv.at[k - 1]).wait()
+        lax.fori_loop(1, n_chip, fill_hand, 0)
+
+        def hand_wait(k, _):
+            hand_copy(k, other).wait_recv()
             return 0
 
-        lax.fori_loop(1, n_scen, fill_wait, 0)
+        lax.fori_loop(0, n_chip, hand_wait, 0)
+        plane_pass_on(1)
 
         row = lax.broadcasted_iota(jnp.int32, (width, width), 0)
         column = lax.broadcasted_iota(jnp.int32, (width, width), 1)
-        on_diagonal = jnp.where(row == column, corner[...], 0.0)
+        whole = corner[...].reshape(width, width)
+        on_diagonal = jnp.where(row == column, whole, 0.0)
         root_row = lax.rsqrt(jnp.sum(on_diagonal, axis=0, keepdims=True))
         root_column = lax.rsqrt(jnp.sum(on_diagonal, axis=1, keepdims=True))
-        scaled = corner[...] * root_column * root_row
+        scaled = whole * root_column * root_row
         high, low = split(scaled)
         scaled_high[...] = high
         scaled_low[...] = low
@@ -443,33 +517,63 @@
         bad = jnp.where(size < SETTLED, 0.0, 1.0)
         y_final = split(y[...])
 
-        @pl.when(me < owners)
+        later = plane_total(1) * root_row
+        late_out[1, 0] = dot3(split(later), y_final, NT)
+        late_to = owners + me * piece // rows
+        late_part = lax.rem(me, rows // piece)
+
+        def late_copy():
+            return pltpu.make_async_remote_copy(
+                src_ref=late_out.at[1, 0],
+                dst_ref=late_out.at[0, late_part],
+                send_sem=late_send,
+                recv_sem=late_recv.at[late_part],
+                device_id={"scen": late_to},
+                device_id_type=pl.DeviceIdType.MESH,
+            )
+
+        @pl.when(late_to != me)
         def _():
-            solve_in[0] = corner[
-                pl.ds(pl.multiple_of(lax.rem(me, owners) * rows, rows), rows), :
-            ]
-
-        @pl.when(me >= owners)
-        def _():
-            for q in range(n_chunk):
-                pltpu.make_async_copy(slots.at[q], slots.at[q], sum_recv.at[q]).wait()
-                solve_in[0, :, pl.ds(q * chunk, chunk)] = own_rows(q)
+            late_copy().start()
 
         rest = solve_in.at[pl.ds(1, n_col - 1)]
         pltpu.make_async_copy(rest, rest, in_recv).wait()
-        given = solve_in[...].reshape(n_col * rows, width) * root_row
-        solved = dot3(split(given), y_final, NT).reshape(n_col, rows, width)
-        solve_out[:, pl.ds(0, rows), :] = solved
-        solve_out[:, pl.ds(rows, 8), :] = jnp.broadcast_to(bad, (n_col, 8, width))
+        given = solve_in[pl.ds(1, n_col - 1)].reshape((n_col - 1) * rows, width) * root_row
+        solved = dot3(split(given), y_final, NT).reshape(n_col - 1, rows, width)
+        solve_out[pl.ds(1, n_col - 1), pl.ds(0, rows), :] = solved
+        solve_out[pl.ds(1, n_col - 1), pl.ds(rows, 8), :] = jnp.broadcast_to(
+            bad, (n_col - 1, 8, width)
+        )
 
         def back_start(k, _):
             back_copy(k).start()
             return 0
 
         lax.fori_loop(1, n_col, back_start, 0)
-        row = me * rows + lax.broadcasted_iota(jnp.int32, (rows, width), 0)
-        column = lax.broadcasted_iota(jnp.int32, (rows, width), 1)
-        out_ref[...] = jnp.where(column <= row, solved[0], 0.0)
+
+        @pl.when(me < owners)
+        def _():
+            chips = rows // piece // 2
+            given = corner[pl.ds(lax.rem(me, owners) * chips, chips)].reshape(rows, width)
+            row = me * rows + lax.broadcasted_iota(jnp.int32, (rows, width), 0)
+            column = lax.broadcasted_iota(jnp.int32, (rows, width), 1)
+            solved = dot3(split(given * root_row), y_final, NT)
+            out_ref[...] = jnp.where(column <= row, solved, 0.0)
+
+        @pl.when(me >= owners)
+        def _():
+            for part in range(rows // piece):
+
+                @pl.when(jnp.logical_and(late_to == me, late_part == part))
+                def _():
+                    out_ref[pl.ds(part * piece, piece), :] = late_out[1, 0]
+
+                @pl.when(jnp.logical_not(jnp.logical_and(late_to == me, late_part == part)))
+                def _():
+                    some = late_out.at[0, part]
+                    pltpu.make_async_copy(some, some, late_recv.at[part]).wait()
+                    out_ref[pl.ds(part * piece, piece), :] = late_out[0, part]
+
         flag_ref[...] = jnp.broadcast_to(bad, flag_ref.shape)
 
         @pl.loop(0, n_chunk * n_sub)
@@ -477,19 +581,18 @@
             ring_copy(0, g).wait_send()
             ring_copy(1, g).wait_send()
 
-        pltpu.make_async_copy(corner_slots, corner_slots, corner_send).wait()
-        pltpu.make_async_copy(corner_slots, corner_slots, fill_send).wait()
-        for q in range(n_chunk):
-
-            @pl.when(me < owners)
-            def _():
-                some = slots.at[q, pl.ds(0, n_scen - owners)]
-                pltpu.make_async_copy(some, some, sum_send.at[q]).wait()
-
-            @pl.when(me >= owners)
-            def _():
-                some = slots.at[q, pl.ds(0, n_scen - owners - 1)]
-                pltpu.make_async_copy(some, some, sum_send.at[q]).wait()
+        for part in range(2):
+            plane_pair_copy(part).wait_send()
+            some = plane_slots.at[part]
+            pltpu.make_async_copy(some, some, plane_send.at[part]).wait()
+        some = corner.at[pl.ds(1, n_chip - 1), 0]
+        pltpu.make_async_copy(some, some, fill_send).wait()
+        some = corner.at[:, 0]
+        pltpu.make_async_copy(some, some, fill_pair_send).wait()
+
+        @pl.when(late_to != me)
+        def _():
+            late_copy().wait_send()
 
         some = solve_out.at[pl.ds(1, n_col - 1)]
         pltpu.make_async_copy(some, some, back_send).wait()
@@ -500,28 +603,13 @@
         coup_rest.wait()
         transpose_coupling(0, block)
 
-        def form(q, r):
-            contribute(q, r * quarter)
-            per = quarter // rows
-
-            def start(k, _):
-                peer = lax.rem(me + k, per) + r * per
-
-                @pl.when(peer != me)
-                def _():
-                    sum_copy(q, peer).start()
-
-                return 0
-
-            lax.fori_loop(0, per, start, 0)
-
-        late = jnp.maximum(z - 1, n_col - 1 - z)
+        late = lag * jnp.maximum(z - 1, n_col - 1 - z)
         n_piece = n_chunk * n_sub
         n_row = block // quarter
 
         @pl.loop(0, n_piece + late)
         def _(t):
-            g = t - (z - 1)
+            g = t - lag * (z - 1)
 
             @pl.when(jnp.logical_and(g >= 0, g < n_piece))
             def _():
@@ -532,7 +620,7 @@
                 def _():
                     up.start()
 
-            h = t - (n_col - 1 - z)
+            h = t - lag * (n_col - 1 - z)
 
             @pl.when(jnp.logical_and(h >= 0, h < n_piece))
             def _():
@@ -552,13 +640,24 @@
             def _():
                 split_prod(q)
 
-            @pl.when(jnp.logical_and(jnp.logical_and(whole, r < n_row), done < n_piece))
+            inside = jnp.logical_and(whole, done < n_piece)
+
+            @pl.when(jnp.logical_and(inside, r < n_row))
             def _():
                 form(q, r)
 
-        @pl.loop(0, n_row)
+            @pl.when(jnp.logical_and(inside, jnp.logical_and(r >= 1, r <= n_row)))
+            def _():
+                pass_on(q, r - 1)
+
+        form(n_chunk - 1, 0)
+
+        @pl.loop(1, n_row)
         def _(r):
             form(n_chunk - 1, r)
+            pass_on(n_chunk - 1, r - 1)
+
+        pass_on(n_chunk - 1, n_row - 1)
 
         for q in range(n_chunk):
             pltpu.make_async_copy(slots.at[q], slots.at[q], sum_recv.at[q]).wait()
@@ -568,6 +667,7 @@
         for q in range(n_chunk):
 
             pltpu.make_async_copy(slots.at[q], slots.at[q], sum_send.at[q]).wait()
+            pltpu.make_async_copy(pair_slots.at[q], pair_slots.at[q], pair_send.at[q]).wait()
         in_copy(z).wait_send()
 
         @pl.loop(0, n_piece)
@@ -585,7 +685,7 @@
         flag_ref[...] = back[pl.ds(rows, 8), pl.ds(0, 128)]
 
 
-def fused(inverses, coupling, tile_mask, hess_diag, quarter=256, chunk=256, sub=128):
+def fused(inverses, coupling, tile_mask, hess_diag, quarter=256, chunk=256, sub=64, lag=3):
     n_scen = lax.axis_size("scen")
     n_col = lax.axis_size("col")
     _, depth, block = coupling.shape
@@ -604,11 +704,13 @@
         vmem((n_chunk, depth, chunk), F32),
         vmem((depth, chunk), BF16),
         vmem((depth, chunk), BF16),
-        vmem((n_chunk, block, chunk), F32),
-        vmem((n_chunk, n_scen - 1, rows, chunk), F32),
-        vmem((width, width), F32),
-        vmem((n_scen - 1, piece, width), F32),
-        vmem((width, width), F32),
+        vmem((n_chunk, n_scen // 2, 2, rows, chunk), F32),
+        vmem((n_chunk, n_scen // 2, rows, chunk), F32),
+        vmem((n_chunk, n_scen // 2 - 1, rows, chunk), F32),
+        vmem((2, n_scen // 2, 2, piece, width), F32),
+        vmem((2, n_scen // 2, piece, width), F32),
+        vmem((2, n_scen // 2 - 1, piece, width), F32),
+        vmem((n_scen // 2, 2, piece, width), F32),
         vmem((width, width), BF16),
         vmem((width, width), BF16),
         vmem((width, width), F32),
@@ -618,22 +720,31 @@
         vmem((n_col, rows, width), F32),
         vmem((n_col, rows + 8, width), F32),
         vmem((rows + 8, width), F32),
+        vmem((2, rows // piece, piece, width), F32),
         dma((3,)),
         dma((2, n_chunk * n_sub)),
         dma((2, n_chunk * n_sub)),
         dma((n_chunk,)),
+        dma((n_chunk, block // quarter)),
         dma((n_chunk,)),
+        dma((n_chunk,)),
+        dma((2,)),
+        dma((2,)),
+        dma((2,)),
+        dma((2,)),
         dma(()),
+        dma((n_scen // 2 - 1,)),
         dma(()),
-        dma(()),
-        dma((n_scen - 1,)),
+        dma((n_scen // 2,)),
         dma(()),
         dma(()),
         dma(()),
         dma(()),
+        dma(()),
+        dma((rows // piece,)),
     ]
     return pl.pallas_call(
-        functools.partial(kernel, n_scen, n_col, quarter, sub),
+        functools.partial(kernel, n_scen, n_col, quarter, sub, lag),
         out_shape=(
             jax.ShapeDtypeStruct((rows, width), F32),
             jax.ShapeDtypeStruct((8, 128), F32),

time: 116 us -> 101 us (0.87); the launches traced: 114 us -> 101 us
  Pallas kernels: 98.6 us -> 85 us
    pallas_call x1, Pallas kernels: 98.6 us -> 85 us  [fused(): pl.pallas_call(functools.partial(kernel, n_scen, n_col, quarter, sub, lag...]
where the time goes in v3:
time: 101 us
  Pallas kernels  85 us (84%)
  between operations  14.1 us (14%)
  local copies, waits for them, and re-layouts  1.15 us (1%)
    pallas_call x1, Pallas kernels, fused(): pl.pallas_call(functools.partial(kernel, n_scen, n_col, quarter, sub, lag...  85 us

profile of v3, /device:TPU:6, one launch (start us, length us, event | category | flops | bytes accessed | tf_op | source)
XLA Modules:
  0.0 100.6 jit_solution(4397418010521854662)
XLA Ops:
  6.5 0.0 copy-start.1
  6.5 0.0 copy-start.2
  6.5 85.0 %shard_map.48 = (f32[32,512]{1,0:T(8,128)S(1)}, f32[8,128]{1,0:T(8,128)S(1)}) custom-call(f32[1,1024,1024]{2,1,0:T(8,128)} %inv_hbm.1, f32[1,1024,1024]{2,1,0:T(8,128)} %coup_hbm.1, s32[1,8]{1,0:T(1,128)} %mask_ref.1, f32[1,512]{1,0:T(1,128)} %bitcast.106), custom_call_target="tpu_custom_call" | custom-call | tf_op jit(solution)/shard_map/pallas_call | solution.py:746
  91.6 0.5 slice.65
  92.7 0.0 copy-done.1
  92.8 0.0 copy-done.2
  92.8 0.3 conditional.1
  93.1 0.6 copy.53
Async XLA Ops:
  6.5 86.2 %copy-start.1 = (f32[512]{0:T(512)S(1)}, f32[512]{0:T(512)}, u32[]{:S(2)}) copy-start(f32[512]{0:T(512)} %param.12) | copy-start | bytes 6148
  6.5 86.2 %copy-start.2 = (s32[1,8]{1,0:T(1,128)S(1)}, s32[1,8]{1,0:T(1,128)}, u32[]{:S(2)}) copy-start(s32[1,8]{1,0:T(1,128)} %mask_ref.1) | copy-start | bytes 100

commit v4 on v3

--- a/solution.py
+++ b/solution.py
@@ -8,20 +8,15 @@
 from jax.sharding import PartitionSpec as P
 
 
-def filled_up(lines, size):
-    spare = -lines.shape[0] % size
-    if not spare:
-        return lines
-    return jnp.concatenate([lines, jnp.zeros((spare, *lines.shape[1:]), lines.dtype)])
-
-
-def spread(x, axis, root):
-    lines = jnp.where(lax.axis_index(axis) == root, x, jnp.zeros_like(x)).reshape(
-        -1, *x.shape[1:][-1:]
-    )
-    padded = filled_up(lines, lax.axis_size(axis))
-    own = lax.psum_scatter(padded, axis, scatter_dimension=0, tiled=True)
-    return lax.all_gather(own, axis, axis=0, tiled=True)[: len(lines)].reshape(x.shape)
+def from_first(x, axis):
+    at = lax.axis_index(axis)
+    have = 1
+    while have < lax.axis_size(axis):
+        pairs = [(i, i + have) for i in range(min(have, lax.axis_size(axis) - have))]
+        got = lax.ppermute(x, axis, pairs)
+        x = jnp.where(jnp.logical_and(at >= have, at < 2 * have), got, x)
+        have *= 2
+    return x
 
 
 def in_blocks(x, dim, size):
@@ -50,10 +45,6 @@
 def collect(x, axis, dim):
     blocks = sent_to_all(x, axis)
     return in_order(blocks, dim)
-
-
-def from_root(x, axis, root):
-    return lax.dynamic_index_in_dim(lax.all_gather(x, axis), root, 0, keepdims=False)
 
 
 def outer_rows(left, piece):
@@ -78,7 +69,7 @@
     scen_size = lax.axis_size("scen")
     rows = local.shape[1] // scen_size
     row_keep = jnp.repeat(tile_mask[0].astype(jnp.float32), local.shape[0] // tile_mask.shape[1])
-    panel = spread(local[:, :width], "col", 0)
+    panel = from_first(local[:, :width], "col")
     panel = panel * row_keep[:, None]
     product = matmul(inverse, panel) * row_keep[:, None]
     block = local
@@ -91,7 +82,7 @@
     def fetch(stacked, low):
         whole = collect(stacked, "scen", 1)
         block = whole[:, low : low + half]
-        return from_root(block, "col", 0)
+        return from_first(block, "col")
 
     identity = jnp.eye(half, dtype=jnp.float32)
     block_one = fetch(schur[None, :, :half], 0)[0]

time: 101 us -> 87.3 us (0.86)
  between operations: 14.1 us -> 0.69 us
where the time goes in v4:
time: 87.3 us; the launch traced here: 87.2 us
  Pallas kernels  85 us (97%)
  local copies, waits for them, and re-layouts  1.15 us (1%)
    pallas_call x1, Pallas kernels, fused(): pl.pallas_call(functools.partial(kernel, n_scen, n_col, quarter, sub, lag...  85 us

profile of v4, /device:TPU:6, one launch (start us, length us, event | category | flops | bytes accessed | tf_op | source)
XLA Modules:
  0.0 87.2 jit_solution(12219216050251709647)
XLA Ops:
  0.0 0.0 copy-start.2
  0.0 0.0 copy-start.3
  0.0 85.0 %shard_map.48 = (f32[32,512]{1,0:T(8,128)S(1)}, f32[8,128]{1,0:T(8,128)S(1)}) custom-call(f32[1,1024,1024]{2,1,0:T(8,128)} %inv_hbm.1, f32[1,1024,1024]{2,1,0:T(8,128)} %coup_hbm.1, s32[1,8]{1,0:T(1,128)} %mask_ref.1, f32[1,512]{1,0:T(1,128)} %bitcast.105), custom_call_target="tpu_custom_call" | custom-call | tf_op jit(solution)/shard_map/pallas_call | solution.py:737
  85.1 0.5 slice.59
  86.2 0.0 copy-done.2
  86.2 0.0 copy-done.3
  86.2 0.3 conditional.1
  86.6 0.6 copy.53
Async XLA Ops:
  0.0 86.2 %copy-start.2 = (f32[512]{0:T(512)S(1)}, f32[512]{0:T(512)}, u32[]{:S(2)}) copy-start(f32[512]{0:T(512)} %param.12) | copy-start | bytes 6148
  0.0 86.2 %copy-start.3 = (s32[1,8]{1,0:T(1,128)S(1)}, s32[1,8]{1,0:T(1,128)}, u32[]{:S(2)}) copy-start(s32[1,8]{1,0:T(1,128)} %mask_ref.1) | copy-start | bytes 100
